TPU v7x, 32 devices: a whole 2x2x4 slice. The times are simulated.
32 devices in a mesh: dp: 4 (over y, x), ctx: 8 (over z, core).
Axes of the slice: x: 2, y: 2, z: 4, core: 2. Of those that a mesh axis runs over, the one named last changes fastest.
Arguments:
- queries: bfloat16 [4, 1024, 1280], P('dp', 'ctx'), may hold values from -16 to 16
- keys: bfloat16 [4, 1024, 1280], P('dp', 'ctx'), may hold values from -16 to 16
- values: bfloat16 [4, 1024, 1280], P('dp', 'ctx'), may hold values from -6 to 6
- seg_lengths: int32 [4, 8], P('dp'), may hold values from 1 to 768, 1024 in all within a row
- out_grad: bfloat16 [4, 1024, 2560], P('dp', 'ctx'), may hold values from -6 to 6
- w_out: bfloat16 [1280, 2560], P('dp'), may hold values from -0.15625 to 0.15625
Outputs:
- attended: bfloat16 [4, 1024, 2560], P('dp', 'ctx')
- query_grad: bfloat16 [4, 1024, 1280], P('dp', 'ctx')
- key_grad: bfloat16 [4, 1024, 1280], P('dp', 'ctx')
- value_grad: bfloat16 [4, 1024, 1280], P('dp', 'ctx')
- w_out_grad: float32 [1280, 2560], P('dp')
Inputs may be any that keep to these rules, and one draw needn't show every extreme that they name: `seg_lengths`: each record's lengths sum to 1024; the longest of each record is exactly 768.
All inputs are finite; a program needn't handle non-finite values.
Results may differ from a plain program's by a relative error of at most 0.027.
Values may be sent and summed in bfloat16 or wider, within the bound.
A program may use at most 192 MiB of HBM per device.

v0:
```python
import math
import jax
import jax.numpy as jnp
from jax import lax
from jax.sharding import PartitionSpec as P

HEADS = 10
HD = 128
MASKED_SCORE = -1e30


def segment_ids(length_row, row_total):
    segment_ends = jnp.cumsum(length_row)
    positions = lax.iota(jnp.int32, row_total)
    return jnp.sum((segment_ends[None, :] <= positions[:, None]).astype(jnp.int32), axis=1)


def head_columns(matrix, head_index, head_width):
    return lax.dynamic_slice_in_dim(matrix, head_index * head_width, head_width, 1)


def take_rows(matrix, first_row, row_count):
    return lax.dynamic_slice_in_dim(matrix, first_row, row_count, 0)


def contract_last(left_side, right_side):
    return lax.dot_general(
        left_side, right_side, (((1,), (1,)), ((), ())), preferred_element_type=jnp.float32
    )


def contract_first(left_side, right_side):
    return lax.dot_general(
        left_side, right_side, (((0,), (0,)), ((), ())), preferred_element_type=jnp.float32
    )


def attend_forward(
    local_query, all_key, all_value, local_segments, all_segments, block_rows, score_scale
):
    local_rows = local_query.shape[0]
    all_rows = all_key.shape[0]
    block_count = all_rows // block_rows

    def one_head(head_index, carried):
        attention, log_norm, stored = carried
        query_head = head_columns(local_query, head_index, HD)
        key_head = head_columns(all_key, head_index, HD)
        value_head = head_columns(all_value, head_index, HD)
        head_scores = contract_last(query_head, key_head) * score_scale

        def block_scores(first_row):
            key_segments = take_rows(all_segments, first_row, block_rows)
            scores = lax.dynamic_slice_in_dim(head_scores, first_row, block_rows, 1)
            return (scores, local_segments[:, None] == key_segments[None, :])

        def stat_step(block_index, running):
            first_row = block_index * block_rows
            row_max, row_sum = running
            scores, same_segment = block_scores(first_row)
            new_max = jnp.maximum(
                row_max, jnp.max(jnp.where(same_segment, scores, MASKED_SCORE), axis=1)
            )
            shifted = jnp.where(same_segment, jnp.exp(scores - new_max[:, None]), 0.0)
            return (new_max, row_sum * jnp.exp(row_max - new_max) + jnp.sum(shifted, axis=1))

        start_state = (
            jnp.full((local_rows,), MASKED_SCORE, jnp.float32),
            jnp.zeros((local_rows,), jnp.float32),
        )
        row_max, row_sum = lax.fori_loop(0, block_count, stat_step, start_state)
        head_norm = row_max + jnp.log(row_sum)

        def value_step(block_index, accumulated):
            first_row = block_index * block_rows
            scores, same_segment = block_scores(first_row)
            soft_weights = jnp.where(
                same_segment, jnp.exp(scores - head_norm[:, None]), 0.0
            ).astype(jnp.bfloat16)
            value_block = take_rows(value_head, first_row, block_rows)
            return accumulated + jnp.dot(
                soft_weights, value_block, preferred_element_type=jnp.float32
            )

        summed = lax.fori_loop(0, block_count, value_step, jnp.zeros((local_rows, HD), jnp.float32))
        attention = lax.dynamic_update_slice_in_dim(
            attention, summed.astype(jnp.bfloat16), head_index * HD, 1
        )
        log_norm = lax.dynamic_update_slice_in_dim(log_norm, head_norm[:, None], head_index, 1)
        stored = lax.dynamic_update_slice_in_dim(stored, head_scores[None], head_index, 0)
        return (attention, log_norm, stored)

    start_triple = (
        jnp.zeros((local_rows, HEADS * HD), jnp.bfloat16),
        jnp.zeros((local_rows, HEADS), jnp.float32),
        jnp.zeros((HEADS, local_rows, all_rows), jnp.float32),
    )
    return lax.fori_loop(0, HEADS, one_head, start_triple)


def attend_backward(
    local_query,
    local_key,
    local_value,
    local_grad,
    local_norm,
    local_dot,
    all_query,
    all_key,
    all_value,
    all_grad,
    all_norm,
    all_dot,
    local_segments,
    all_segments,
    stored,
    block_rows,
    score_scale,
):
    local_rows = local_query.shape[0]
    block_count = all_key.shape[0] // block_rows

    def one_head(head_index, carried):
        query_grad, key_grad, value_grad = carried
        grad_head = head_columns(local_grad, head_index, HD)
        own_key = head_columns(local_key, head_index, HD)
        own_value = head_columns(local_value, head_index, HD)
        key_head = head_columns(all_key, head_index, HD)
        value_head = head_columns(all_value, head_index, HD)
        query_all = head_columns(all_query, head_index, HD)
        grad_all = head_columns(all_grad, head_index, HD)
        norm_head = head_columns(local_norm, head_index, 1)[:, 0]
        dot_head = head_columns(local_dot, head_index, 1)[:, 0]
        norm_all = head_columns(all_norm, head_index, 1)[:, 0]
        dot_all = head_columns(all_dot, head_index, 1)[:, 0]
        head_scores = lax.dynamic_index_in_dim(stored, head_index, 0, keepdims=False)

        def query_step(block_index, accumulated):
            first_row = block_index * block_rows
            key_segments = take_rows(all_segments, first_row, block_rows)
            key_block = take_rows(key_head, first_row, block_rows)
            value_block = take_rows(value_head, first_row, block_rows)
            scores = lax.dynamic_slice_in_dim(head_scores, first_row, block_rows, 1)
            same_segment = local_segments[:, None] == key_segments[None, :]
            probs = jnp.where(same_segment, jnp.exp(scores - norm_head[:, None]), 0.0)
            dprob = contract_last(grad_head, value_block)
            dscore = (probs * (dprob - dot_head[:, None])).astype(jnp.bfloat16)
            return accumulated + jnp.dot(dscore, key_block, preferred_element_type=jnp.float32)

        query_sum = lax.fori_loop(
            0, block_count, query_step, jnp.zeros((local_rows, HD), jnp.float32)
        )

        def key_step(block_index, running):
            first_row = block_index * block_rows
            query_segments = take_rows(all_segments, first_row, block_rows)
            key_sum, value_sum = running
            query_block = take_rows(query_all, first_row, block_rows)
            grad_block = take_rows(grad_all, first_row, block_rows)
            norm_block = take_rows(norm_all, first_row, block_rows)
            dot_block = take_rows(dot_all, first_row, block_rows)
            scores = contract_last(query_block, own_key) * score_scale
            same_segment = query_segments[:, None] == local_segments[None, :]
            probs = jnp.where(same_segment, jnp.exp(scores - norm_block[:, None]), 0.0)
            dprob = contract_last(grad_block, own_value)
            dscore = (probs * (dprob - dot_block[:, None])).astype(jnp.bfloat16)
            key_sum = key_sum + contract_first(dscore, query_block)
            value_sum = value_sum + contract_first(probs.astype(jnp.bfloat16), grad_block)
            return (key_sum, value_sum)

        zeros = jnp.zeros((local_rows, HD), jnp.float32)
        key_sum, value_sum = lax.fori_loop(0, block_count, key_step, (zeros, zeros))
        query_grad = lax.dynamic_update_slice_in_dim(
            query_grad, (query_sum * score_scale).astype(jnp.bfloat16), head_index * HD, 1
        )
        key_grad = lax.dynamic_update_slice_in_dim(
            key_grad, (key_sum * score_scale).astype(jnp.bfloat16), head_index * HD, 1
        )
        value_grad = lax.dynamic_update_slice_in_dim(
            value_grad, value_sum.astype(jnp.bfloat16), head_index * HD, 1
        )
        return (query_grad, key_grad, value_grad)

    empty = jnp.zeros((local_rows, HEADS * HD), jnp.bfloat16)
    return lax.fori_loop(0, HEADS, one_head, (empty, empty, empty))


def local(queries, keys, values, seg_lengths, out_grad, w_out):
    score_scale = 1.0 / math.sqrt(HD)
    local_rows = queries.shape[1]
    all_rows = local_rows * lax.axis_size("ctx")
    block_rows = min(all_rows, 512)
    local_query = queries[0]
    local_key = keys[0]
    local_value = values[0]
    local_outgrad = out_grad[0]
    all_segments = segment_ids(seg_lengths[0], all_rows)
    local_segments = take_rows(all_segments, lax.axis_index("ctx") * local_rows, local_rows)
    full_weight = lax.all_gather(w_out, "dp", axis=0, tiled=True)
    attn_grad = contract_last(local_outgrad, full_weight).astype(jnp.bfloat16)
    all_key, all_value, all_query, all_grad = (
        lax.all_gather(local_key, "ctx", axis=0, tiled=True),
        lax.all_gather(local_value, "ctx", axis=0, tiled=True),
        lax.all_gather(local_query, "ctx", axis=0, tiled=True),
        lax.all_gather(attn_grad, "ctx", axis=0, tiled=True),
    )
    attention, log_norm, stored = attend_forward(
        local_query, all_key, all_value, local_segments, all_segments, block_rows, score_scale
    )
    attended = jnp.dot(attention, full_weight, preferred_element_type=jnp.float32).astype(
        jnp.bfloat16
    )
    products = attn_grad.astype(jnp.float32) * attention.astype(jnp.float32)
    grad_dot = jnp.sum(products.reshape(local_rows, HEADS, HD), axis=2)
    all_norm, all_dot = (
        lax.all_gather(log_norm, "ctx", axis=0, tiled=True),
        lax.all_gather(grad_dot, "ctx", axis=0, tiled=True),
    )
    query_grad, key_grad, value_grad = attend_backward(
        local_query,
        local_key,
        local_value,
        attn_grad,
        log_norm,
        grad_dot,
        all_query,
        all_key,
        all_value,
        all_grad,
        all_norm,
        all_dot,
        local_segments,
        all_segments,
        stored,
        block_rows,
        score_scale,
    )
    grad_share = lax.psum_scatter(
        contract_first(attention, local_outgrad).astype(jnp.bfloat16),
        "dp",
        scatter_dimension=0,
        tiled=True,
    )
    weight_grad = lax.psum(grad_share, "ctx").astype(jnp.float32)
    return (attended[None], query_grad[None], key_grad[None], value_grad[None], weight_grad)


def solution(mesh):
    in_specs = (
        P("dp", "ctx", None),
        P("dp", "ctx", None),
        P("dp", "ctx", None),
        P("dp", None),
        P("dp", "ctx", None),
        P("dp", None),
    )
    out_specs = (
        P("dp", "ctx", None),
        P("dp", "ctx", None),
        P("dp", "ctx", None),
        P("dp", "ctx", None),
        P("dp", None),
    )
    return jax.shard_map(local, mesh=mesh, in_specs=in_specs, out_specs=out_specs, check_vma=False)
```

profile of v0, /device:TPU:0, one launch (start us, length us, event | category | flops | bytes accessed | tf_op | source)
XLA Modules:
  0.0 421.3 jit_solution(8447683285333391024)
XLA Ops:
  10.5 35.8 %all-gather.13.cloned.1.call-done = bf16[1,1024,1280]{2,1,0:T(8,128)(2,1)} async-done(((bf16[1,128,1280]{2,1,0:T(8,128)(2,1)}), bf16[1,1024,1280]{2,1,0:T(8,128)(2,1)}) %all-gather.13.cloned.1.call-update) | async-done | bytes 2621456 | tf_op jit(solution)/shard_map/all_gather | solution.py:202
  46.3 34.5 %all-gather.15.cloned.1.call-done = bf16[1,1024,1280]{2,1,0:T(8,128)(2,1)} async-done(((bf16[1,128,1280]{2,1,0:T(8,128)(2,1)}), bf16[1,1024,1280]{2,1,0:T(8,128)(2,1)}) %all-gather.15.cloned.1.call-update) | async-done | bytes 2621456 | tf_op jit(solution)/shard_map/all_gather | solution.py:203
  80.8 48.7 %while.152 = (s32[]{:T(128)}, bf16[128,1280]{1,0:T(8,128)(2,1)S(1)}, f32[128,10]{0,1:T(8,128)S(1)}, f32[10,128,1024]{2,1,0:T(8,128)}, bf16[128,1280]{1,0:T(8,128...) while((s32[]{:T(128)}, bf16[128,1280]{1,0:T(8,128)(2,1)S(1)}, ...), condition=%wide.region_9.10_spmd, body=%wide.region_2.9_spmd.sunk | while | flops 51233556 | bytes 3044121 | solution.py:98
  80.9 2.0 bitcast_dynamic-update-slice_fusion.2
  82.9 1.0 while.156
  85.7 2.0 bitcast_dynamic-update-slice_fusion.2
  87.8 1.0 while.156
  88.8 1.0 constant_dynamic-slice_fusion.26
  90.7 2.0 bitcast_dynamic-update-slice_fusion.2
  92.7 1.0 while.156
  95.5 2.0 bitcast_dynamic-update-slice_fusion.2
  97.5 1.0 while.156
  100.4 2.0 bitcast_dynamic-update-slice_fusion.2
  102.4 1.0 while.156
  105.3 2.0 bitcast_dynamic-update-slice_fusion.2
  107.3 1.0 while.156
  110.1 2.0 bitcast_dynamic-update-slice_fusion.2
  112.2 1.0 while.156
  115.0 2.0 bitcast_dynamic-update-slice_fusion.2
  117.0 1.0 while.156
  119.9 2.0 bitcast_dynamic-update-slice_fusion.2
  121.9 1.0 while.156
  124.7 2.0 bitcast_dynamic-update-slice_fusion.2
  129.6 4.6 %convolution_convert_fusion = bf16[1280,2560]{1,0:T(8,128)(2,1)} fusion(bf16[128,1280]{1,0:T(8,128)(2,1)S(1)} %get-tuple-element.1124, bf16[1,128,2560]{2,1,0:T(8,128)(2,1)S(1)} %copy-done), kind=kOutput, calls=%fused_computation.82 | convolution fusion | flops 842137600 | bytes 7536640 | tf_op jit(solution)/shard_map/dot_general | solution.py:33
  134.9 19.2 %all-gather.9.cloned.1.call-done = bf16[1280,2560]{1,0:T(8,128)(2,1)} async-done(((bf16[320,2560]{1,0:T(8,128)(2,1)}), bf16[1280,2560]{1,0:T(8,128)(2,1)}) %all-gather.9.cloned.1.call-update) | async-done | bytes 6553616 | tf_op jit(solution)/shard_map/all_gather | solution.py:199
  154.1 5.8 %convert_multiply_fusion = (f32[128,1280]{1,0:T(8,128)S(1)}, bf16[128,1280]{1,0:T(8,128)(2,1)}) fusion(bf16[128,1280]{1,0:T(8,128)(2,1)S(1)} %get-tuple-element.1124, bf16[1280,2560]{1,0:T(8,128)(2,1)} %all-gather.9.cloned.1.call-done, bf16[1,128,2560]{2,1,0:T(8,128)(2,1)S(1)} %copy-done), kind=kOutput, calls=%fused_computation.88 | convolution fusion | flops 839516160 | bytes 8519680 | tf_op jit(solution)/shard_map/dot_general | solution.py:27
  159.9 14.0 %all_gather.26 = f32[1024,10]{0,1:T(8,128)S(1)} all-gather(f32[128,10]{0,1:T(8,128)S(1)} %get-tuple-element.2072), channel_id=1, replica_groups=mesh['dp'=4,'ctx'=8] {'ctx'}, dimensions={0}, use_global_device_ids=true | all-gather | bytes 46080 | tf_op jit(solution)/shard_map/all_gather | solution.py:216
  174.2 13.9 %all_gather.27 = f32[1024,10]{0,1:T(8,128)S(1)} all-gather(f32[128,10]{0,1:T(8,128)S(1)} %reduce_sum.32), channel_id=1, replica_groups=mesh['dp'=4,'ctx'=8] {'ctx'}, dimensions={0}, use_global_device_ids=true | all-gather | bytes 46080 | tf_op jit(solution)/shard_map/all_gather | solution.py:217
  188.2 4.9 %fusion.56 = bf16[1,128,2560]{2,1,0:T(8,128)(2,1)} fusion(bf16[128,1280]{1,0:T(8,128)(2,1)S(1)} %get-tuple-element.1124, bf16[1280,2560]{1,0:T(8,128)(2,1)} %all-gather.9.cloned.1.call-done), kind=kOutput, calls=%fused_computation.84 | convolution fusion | flops 839188480 | bytes 7536640 | tf_op jit(solution)/shard_map/dot_general | solution.py:210
  193.0 36.4 %reduce-scatter.2.cloned.1.call-done = bf16[320,2560]{1,0:T(8,128)(2,1)} async-done(((bf16[1280,2560]{1,0:T(8,128)(2,1)}), bf16[320,2560]{1,0:T(8,128)(2,1)}) %reduce-scatter.2.cloned.1.call-update) | async-done | bytes 1638416 | tf_op jit(solution)/shard_map/reduce_scatter | solution.py:238
  229.4 35.4 %all-gather.17.cloned.1.call-done = bf16[1,1024,1280]{2,1,0:T(8,128)(2,1)} async-done(((bf16[1,128,1280]{2,1,0:T(8,128)(2,1)}), bf16[1,1024,1280]{2,1,0:T(8,128)(2,1)}) %all-gather.17.cloned.1.call-update) | async-done | bytes 2621456 | tf_op jit(solution)/shard_map/all_gather | solution.py:204
  264.8 35.0 %all-gather.11.cloned.1.call-done = bf16[1024,1280]{1,0:T(8,128)(2,1)} async-done(((bf16[128,1280]{1,0:T(8,128)(2,1)}), bf16[1024,1280]{1,0:T(8,128)(2,1)}) %all-gather.11.cloned.1.call-update) | async-done | bytes 2621456 | tf_op jit(solution)/shard_map/all_gather | solution.py:205
  299.9 110.6 %while.155 = (s32[]{:T(128)}, bf16[128,1280]{1,0:T(8,128)(2,1)S(1)}, bf16[128,1280]{1,0:T(8,128)(2,1)S(1)}, bf16[128,1280]{1,0:T(8,128)(2,1)S(1)}, bf16[1024,128...) while((s32[]{:T(128)}, bf16[128,1280]{1,0:T(8,128)(2,1)S(1)}, ...), condition=%wide.region_16.17_spmd, body=%wide.region_11.16_spmd.sunk | while | flops 101761040 | bytes 7062036 | solution.py:185
  299.9 1.1 constant_dynamic-slice_fusion.27
  303.9 1.1 while.158
  308.5 2.3 while.159
  311.0 1.1 constant_dynamic-slice_fusion.27
  315.0 1.1 while.158
  319.6 2.3 while.159
  322.0 1.1 constant_dynamic-slice_fusion.27
  326.1 1.1 while.158
  330.7 2.3 while.159
  333.1 1.1 constant_dynamic-slice_fusion.27
  337.1 1.1 while.158
  341.7 2.3 while.159
  344.2 1.1 constant_dynamic-slice_fusion.27
  348.2 1.1 while.158
  352.8 2.3 while.159
  355.2 1.1 constant_dynamic-slice_fusion.27
  359.3 1.1 while.158
  363.9 2.3 while.159
  366.3 1.1 constant_dynamic-slice_fusion.27
  370.3 1.1 while.158
  374.9 2.3 while.159
  377.4 1.1 constant_dynamic-slice_fusion.27
  381.4 1.1 while.158
  386.0 2.3 while.159
  388.4 1.1 constant_dynamic-slice_fusion.27
  392.4 1.1 while.158
  397.0 2.3 while.159
  399.5 1.1 constant_dynamic-slice_fusion.27
  403.5 1.1 while.158
  408.1 2.3 while.159
  410.6 3.8 convert_element_type.83
  (604 shorter events, 135.2 us)
Async XLA Ops:
  7.2 122.4 %copy-start = (bf16[1,128,2560]{2,1,0:T(8,128)(2,1)S(1)}, bf16[1,128,2560]{2,1,0:T(8,128)(2,1)}, u32[]{:S(2)}) copy-start(bf16[1,128,2560]{2,1,0:T(8,128)(2,1)} %param.22) | copy-start | bytes 1966084
  7.2 39.1 %all-gather.13.cloned.1.call-start = ((), (), s32[]{:S(2)}) async-start(), calls=%async_computation.5 | async-start | bytes 2949120 | tf_op jit(solution)/shard_map/all_gather | solution.py:202
  7.9 72.9 %all-gather.15.cloned.1.call-start = ((), (), s32[]{:S(2)}) async-start(), calls=%async_computation.6 | async-start | bytes 2949120 | tf_op jit(solution)/shard_map/all_gather | solution.py:203
  8.7 145.4 %all-gather.9.cloned.1.call-start = ((), (), s32[]{:S(2)}) async-start(), calls=%async_computation.1 | async-start | bytes 8192000 | tf_op jit(solution)/shard_map/all_gather | solution.py:199
  9.4 220.0 %reduce-scatter.2.cloned.1.call-start = ((), (), s32[]{:S(2)}) async-start(), calls=%async_computation.3 | async-start | bytes 8192000 | tf_op jit(solution)/shard_map/reduce_scatter | solution.py:238
  134.2 130.6 %all-gather.17.cloned.1.call-start = ((), (), s32[]{:S(2)}) async-start(), calls=%async_computation.7 | async-start | bytes 2949120 | tf_op jit(solution)/shard_map/all_gather | solution.py:204
  134.8 165.0 %all-gather.11.cloned.1.call-start = ((), (), s32[]{:S(2)}) async-start(), calls=%async_computation.2 | async-start | bytes 2949120 | tf_op jit(solution)/shard_map/all_gather | solution.py:205
  159.9 250.7 %all-reduce.2.cloned.1.call-start = ((), (), s32[]{:S(2)}) async-start(), calls=%async_computation.4 | async-start | bytes 3276800 | tf_op jit(solution)/shard_map/psum | solution.py:244
  410.5 3.9 copy-start.1
  410.5 3.9 copy-start.2
  410.5 3.9 copy-start.3
Sparse Core Ops, SparseCore 0:
  9.7 36.5 all-gather.12
  47.9 32.8 all-gather.14
  82.7 71.3 all-gather.8
  157.0 72.3 reduce-scatter.1
  230.9 33.8 all-gather.16
  266.9 32.8 all-gather.10
  302.2 61.1 all-reduce.1
where the time goes:
time: 426 us; the launch traced here: 421 us
  waiting for transfers between devices  199 us (47%)
  local copies, waits for them, and re-layouts  94.9 us (22%)
  matrix products  66.7 us (16%)
  blocking collectives  28 us (7%)
  between operations  14.3 us (3%)
  other arithmetic  13.7 us (3%)
  loops' own time  4.48 us (1%)
    dynamic_slice x120, local copies, waits for them, and re-layouts, head_columns(): lax.dynamic_slice_in_dim(matrix, head_index * head_width, head_width, 1)  72.1 us
    reduce_scatter x1, waiting for transfers between devices, local(): lax.psum_scatter(contract_first(attention, local_outgrad).astype(jnp.bflo...  36.4 us
    all_gather x1, waiting for transfers between devices, local(): lax.all_gather(local_key, 'ctx', axis=0, tiled=True)  35.8 us
    all_gather x1, waiting for transfers between devices, local(): lax.all_gather(local_query, 'ctx', axis=0, tiled=True)  35.4 us
    all_gather x1, waiting for transfers between devices, local(): lax.all_gather(attn_grad, 'ctx', axis=0, tiled=True)  35 us
    all_gather x1, waiting for transfers between devices, local(): lax.all_gather(local_value, 'ctx', axis=0, tiled=True)  34.5 us
    dot_general x31, matrix products, contract_last(): lax.dot_general(left_side, right_side, (((1,), (1,)), ((), ())), preferre...  30.4 us
    all_gather x1, waiting for transfers between devices, local(): full_weight = lax.all_gather(w_out, 'dp', axis=0, tiled=True)  19.2 us
  transfers between devices with their start and end apart: 7, of which 6 were waited for; matrix products, arithmetic and copies ran while one was open for 41% of the time, Pallas kernels for 0%

commit v1 on v0

--- a/solution.py
+++ b/solution.py
@@ -7,6 +7,17 @@
 HEADS = 10
 HD = 128
 MASKED_SCORE = -1e30
+
+
+def gather_by_hops(x, mesh_axis, dim):
+    size = lax.axis_size(mesh_axis)
+    hops = [(i, (i + 1) % size) for i in range(size)]
+    parts = [x]
+    for reach in range(1, size):
+        parts = [lax.ppermute(parts[0], mesh_axis, hops), *parts]
+    whole = jnp.concatenate(parts, axis=dim)
+    shift = (lax.axis_index(mesh_axis) + 1) * parts[-1].shape[dim]
+    return jnp.roll(whole, shift, axis=dim)
 
 
 def segment_ids(length_row, row_total):
@@ -196,7 +207,7 @@
     local_outgrad = out_grad[0]
     all_segments = segment_ids(seg_lengths[0], all_rows)
     local_segments = take_rows(all_segments, lax.axis_index("ctx") * local_rows, local_rows)
-    full_weight = lax.all_gather(w_out, "dp", axis=0, tiled=True)
+    full_weight = gather_by_hops(w_out, "dp", 0)
     attn_grad = contract_last(local_outgrad, full_weight).astype(jnp.bfloat16)
     all_key, all_value, all_query, all_grad = (
         lax.all_gather(local_key, "ctx", axis=0, tiled=True),

time: 426 us -> 473 us (1.11)
  waiting for transfers between devices: 199 us -> 233 us
  local copies, waits for them, and re-layouts: 94.9 us -> 107 us
    ppermute x0 -> x3, waiting for transfers between devices: none -> 159 us  [gather_by_hops(): parts = [lax.ppermute(parts[0], mesh_axis, hops), *parts]]
    reduce_scatter x1, waiting for transfers between devices: 36.4 us -> 0.01 us  [local(): lax.psum_scatter(contract_first(attention, local_outgrad).astype(jnp.bflo...]
    all_gather x1, waiting for transfers between devices: 35.4 us -> 0.02 us  [local(): lax.all_gather(local_query, 'ctx', axis=0, tiled=True)]
    all_gather x1, waiting for transfers between devices: 35 us -> 1.74 us  [local(): lax.all_gather(attn_grad, 'ctx', axis=0, tiled=True)]
    all_gather x1 -> x0, waiting for transfers between devices: 19.2 us -> none  [local(): full_weight = lax.all_gather(w_out, 'dp', axis=0, tiled=True)]
    dynamic_slice x20 -> x0, local copies, waits for them, and re-layouts: 12.8 us -> none  [one_head(): lax.dynamic_index_in_dim(stored, head_index, 0, keepdims=False)]
    unnamed x8 -> x23, local copies, waits for them, and re-layouts: 0.03 us -> 12.4 us
    squeeze x0 -> x10, local copies, waits for them, and re-layouts: none -> 10.9 us  [one_head(): lax.dynamic_index_in_dim(stored, head_index, 0, keepdims=False)]
  transfers between devices with their start and end apart: 7 -> 9, of which waited for: 6 -> 6; matrix products, arithmetic and copies ran while one was open for 41% -> 26% of each run, Pallas kernels for 0% -> 0%
where the time goes in v1:
time: 473 us; the launch traced here: 468 us
  waiting for transfers between devices  233 us (49%)
  local copies, waits for them, and re-layouts  107 us (23%)
  matrix products  63.4 us (13%)
  blocking collectives  28.2 us (6%)
  between operations  14.4 us (3%)
  other arithmetic  13.7 us (3%)
  loops' own time  4.77 us (1%)
    ppermute x3, waiting for transfers between devices, gather_by_hops(): parts = [lax.ppermute(parts[0], mesh_axis, hops), *parts]  159 us
    dynamic_slice x130, local copies, waits for them, and re-layouts, head_columns(): lax.dynamic_slice_in_dim(matrix, head_index * head_width, head_width, 1)  73.3 us
    all_gather x1, waiting for transfers between devices, local(): lax.all_gather(local_key, 'ctx', axis=0, tiled=True)  36.5 us
    all_gather x1, waiting for transfers between devices, local(): lax.all_gather(local_value, 'ctx', axis=0, tiled=True)  34.5 us
    dot_general x31, matrix products, contract_last(): lax.dot_general(left_side, right_side, (((1,), (1,)), ((), ())), preferre...  27.3 us
    dot_general x41, matrix products, contract_first(): lax.dot_general(left_side, right_side, (((0,), (0,)), ((), ())), preferre...  18.4 us
    all_gather x1, blocking collectives, local(): lax.all_gather(grad_dot, 'ctx', axis=0, tiled=True)  14.1 us
    all_gather x1, blocking collectives, local(): lax.all_gather(log_norm, 'ctx', axis=0, tiled=True)  14.1 us
  transfers between devices with their start and end apart: 9, of which 6 were waited for; matrix products, arithmetic and copies ran while one was open for 26% of the time, Pallas kernels for 0%

profile of v1, /device:TPU:0, one launch (start us, length us, event | category | flops | bytes accessed | tf_op | source)
XLA Modules:
  0.0 468.5 jit_solution(12447787833063976131)
XLA Ops:
  9.7 36.5 %all-gather.10.cloned.1.call-done = bf16[1,1024,1280]{2,1,0:T(8,128)(2,1)} async-done(((bf16[1,128,1280]{2,1,0:T(8,128)(2,1)}), bf16[1,1024,1280]{2,1,0:T(8,128)(2,1)}) %all-gather.10.cloned.1.call-update) | async-done | bytes 2621456 | tf_op jit(solution)/shard_map/all_gather | solution.py:213
  46.3 34.5 %all-gather.12.cloned.1.call-done = bf16[1,1024,1280]{2,1,0:T(8,128)(2,1)} async-done(((bf16[1,128,1280]{2,1,0:T(8,128)(2,1)}), bf16[1,1024,1280]{2,1,0:T(8,128)(2,1)}) %all-gather.12.cloned.1.call-update) | async-done | bytes 2621456 | tf_op jit(solution)/shard_map/all_gather | solution.py:214
  80.8 48.6 %while.152 = (s32[]{:T(128)}, bf16[128,1280]{1,0:T(8,128)(2,1)S(1)}, f32[128,10]{0,1:T(8,128)S(1)}, f32[10,128,1024]{2,1,0:T(8,128)}, bf16[128,1280]{1,0:T(8,128...) while((s32[]{:T(128)}, bf16[128,1280]{1,0:T(8,128)(2,1)S(1)}, ...), condition=%wide.region_9.10_spmd, body=%wide.region_2.9_spmd.sunk | while | flops 51233556 | bytes 3044097 | solution.py:109
  80.9 2.0 bitcast_dynamic-update-slice_fusion.2
  82.9 1.0 while.156
  85.7 2.0 bitcast_dynamic-update-slice_fusion.2
  87.7 1.0 while.156
  90.6 2.0 bitcast_dynamic-update-slice_fusion.2
  92.6 1.0 while.156
  95.4 2.0 bitcast_dynamic-update-slice_fusion.2
  97.4 1.0 while.156
  100.3 2.0 bitcast_dynamic-update-slice_fusion.2
  102.3 1.0 while.156
  105.1 2.0 bitcast_dynamic-update-slice_fusion.2
  107.2 1.0 while.156
  110.0 2.0 bitcast_dynamic-update-slice_fusion.2
  112.0 1.0 while.156
  114.9 2.0 bitcast_dynamic-update-slice_fusion.2
  116.9 1.0 while.156
  119.7 2.0 bitcast_dynamic-update-slice_fusion.2
  121.7 1.0 while.156
  124.6 2.0 bitcast_dynamic-update-slice_fusion.2
  126.6 1.0 while.156
  129.5 4.6 convolution_convert_fusion
  134.1 1.5 collective-permute-start
  135.6 68.3 %collective-permute-done = bf16[320,2560]{1,0:T(8,128)(2,1)S(1)} collective-permute-done((bf16[320,2560]{1,0:T(8,128)(2,1)S(1)}, bf16[320,2560]{1,0:T(8,128)(2,1)S(1)}, u32[]{:S(2)}, u32[]{:S(2)}) %collective-permute-start) | collective-permute-done | bytes 1638432 | tf_op jit(solution)/shard_map/ppermute | solution.py:17
  203.9 1.2 copy-done.2
  205.1 1.7 collective-permute-start.1
  206.8 54.1 %collective-permute-done.1 = bf16[320,2560]{1,0:T(8,128)(2,1)} collective-permute-done((bf16[320,2560]{1,0:T(8,128)(2,1)S(1)}, bf16[320,2560]{1,0:T(8,128)(2,1)}, u32[]{:S(2)}, u32[]{:S(2)}) %collective-permute-start.1) | collective-permute-done | bytes 1638432 | tf_op jit(solution)/shard_map/ppermute | solution.py:17
  261.8 36.6 %collective-permute-done.2 = bf16[320,2560]{1,0:T(8,128)(2,1)} collective-permute-done((bf16[320,2560]{1,0:T(8,128)(2,1)}, bf16[320,2560]{1,0:T(8,128)(2,1)}, u32[]{:S(2)}, u32[]{:S(2)}) %collective-permute-start.2) | collective-permute-done | bytes 1638432 | tf_op jit(solution)/shard_map/ppermute | solution.py:17
  298.4 1.5 constant_dynamic-update-slice_fusion.7
  300.0 1.5 constant_dynamic-update-slice_fusion.6
  301.8 1.5 constant_dynamic-update-slice_fusion.3
  303.3 1.5 constant_dynamic-update-slice_fusion.2
  305.1 4.7 %copy-done.4 = bf16[2560,2560]{1,0:T(8,128)(2,1)} copy-done((bf16[2560,2560]{1,0:T(8,128)(2,1)}, bf16[2560,2560]{1,0:T(8,128)(2,1)S(1)}, u32[]{:S(2)}) %copy-start.4) | copy-done | bytes 13107224
  309.8 2.7 convert_multiply_fusion
  312.5 14.1 %all_gather.22 = f32[1024,10]{0,1:T(8,128)S(1)} all-gather(f32[128,10]{0,1:T(8,128)S(1)} %get-tuple-element.2090), channel_id=1, replica_groups=mesh['dp'=4,'ctx'=8] {'ctx'}, dimensions={0}, use_global_device_ids=true | all-gather | bytes 46080 | tf_op jit(solution)/shard_map/all_gather | solution.py:227
  326.6 14.1 %all_gather.23 = f32[1024,10]{0,1:T(8,128)S(1)} all-gather(f32[128,10]{0,1:T(8,128)S(1)} %reduce_sum.32), channel_id=1, replica_groups=mesh['dp'=4,'ctx'=8] {'ctx'}, dimensions={0}, use_global_device_ids=true | all-gather | bytes 46080 | tf_op jit(solution)/shard_map/all_gather | solution.py:228
  340.8 5.9 %fusion.63 = bf16[1,128,2560]{2,1,0:T(8,128)(2,1)} fusion(bf16[128,1280]{1,0:T(8,128)(2,1)S(1)} %get-tuple-element.1124, bf16[2560,2560]{1,0:T(8,128)(2,1)} %copy-done.4, s32[]{:T(128)S(6)} %select_n.135), kind=kOutput, calls=%fused_computation.88 | convolution fusion | flops 839188480 | bytes 7536644 | tf_op jit(solution)/shard_map/dot_general | solution.py:221
  346.7 1.7 all-gather.8.cloned.1.call-done
  348.5 109.2 %while.155 = (s32[]{:T(128)}, bf16[128,1280]{1,0:T(8,128)(2,1)S(1)}, bf16[128,1280]{1,0:T(8,128)(2,1)S(1)}, bf16[128,1280]{1,0:T(8,128)(2,1)S(1)}, bf16[1024,128...) while((s32[]{:T(128)}, bf16[128,1280]{1,0:T(8,128)(2,1)S(1)}, ...), condition=%wide.region_16.17_spmd, body=%wide.region_11.16_spmd.sunk | while | flops 101761040 | bytes 6078972 | solution.py:196
  351.4 1.1 dynamic-slice_bitcast_fusion.2
  353.4 1.0 constant_dynamic-slice_fusion.30
  357.0 2.4 while.159
  362.3 1.1 dynamic-slice_bitcast_fusion.2
  367.9 2.4 while.159
  373.2 1.1 dynamic-slice_bitcast_fusion.2
  378.8 2.4 while.159
  384.1 1.1 dynamic-slice_bitcast_fusion.2
  386.2 1.0 constant_dynamic-slice_fusion.30
  389.8 2.4 while.159
  395.1 1.1 dynamic-slice_bitcast_fusion.2
  400.7 2.4 while.159
  406.0 1.1 dynamic-slice_bitcast_fusion.2
  411.6 2.4 while.159
  416.9 1.1 dynamic-slice_bitcast_fusion.2
  422.5 2.4 while.159
  427.8 1.1 dynamic-slice_bitcast_fusion.2
  433.4 2.4 while.159
  438.7 1.1 dynamic-slice_bitcast_fusion.2
  444.3 2.4 while.159
  449.7 1.1 dynamic-slice_bitcast_fusion.2
  455.2 2.4 while.159
  457.8 3.8 convert_element_type.87
  (623 shorter events, 140.2 us)
Async XLA Ops:
  7.2 122.3 %copy-start = (bf16[1,128,2560]{2,1,0:T(8,128)(2,1)S(1)}, bf16[1,128,2560]{2,1,0:T(8,128)(2,1)}, u32[]{:S(2)}) copy-start(bf16[1,128,2560]{2,1,0:T(8,128)(2,1)} %param.22) | copy-start | bytes 1966084
  7.2 39.1 %all-gather.10.cloned.1.call-start = ((), (), s32[]{:S(2)}) async-start(), calls=%async_computation.4 | async-start | bytes 2949120 | tf_op jit(solution)/shard_map/all_gather | solution.py:213
  7.9 72.9 %all-gather.12.cloned.1.call-start = ((), (), s32[]{:S(2)}) async-start(), calls=%async_computation.5 | async-start | bytes 2949120 | tf_op jit(solution)/shard_map/all_gather | solution.py:214
  8.7 338.0 %reduce-scatter.2.cloned.1.call-start = ((), (), s32[]{:S(2)}) async-start(), calls=%async_computation.2 | async-start | bytes 8192000 | tf_op jit(solution)/shard_map/reduce_scatter | solution.py:249
  129.5 4.7 copy-start.1
  134.1 212.6 %all-gather.14.cloned.1.call-start = ((), (), s32[]{:S(2)}) async-start(), calls=%async_computation.6 | async-start | bytes 2949120 | tf_op jit(solution)/shard_map/all_gather | solution.py:215
  134.1 69.8 %collective-permute-start = (bf16[320,2560]{1,0:T(8,128)(2,1)S(1)}, bf16[320,2560]{1,0:T(8,128)(2,1)S(1)}, u32[]{:S(2)}, u32[]{:S(2)}) collective-permute-start(bf16[320,2560]{1,0:T(8,128)(2,1)S(1)} %copy-done.1), channel_id=1, source_target_pairs={{0,8},{8,16},{16,24},{24,0},{1,9},{9,17},{17,25},{25,1},{2,10},{10... | collective-permute-start | bytes 4915208 | tf_op jit(solution)/shard_map/ppermute | solution.py:17
  203.9 1.2 copy-start.2
  205.1 55.8 %collective-permute-start.1 = (bf16[320,2560]{1,0:T(8,128)(2,1)S(1)}, bf16[320,2560]{1,0:T(8,128)(2,1)}, u32[]{:S(2)}, u32[]{:S(2)}) collective-permute-start(bf16[320,2560]{1,0:T(8,128)(2,1)S(1)} %collective-permute-done), channel_id=1, source_target_pairs={{0,8},{8,16},{16,24},{24,0},{1,9},{9,17},{17,25},{25,1},{2,10},{10... | collective-permute-start | bytes 4915208 | tf_op jit(solution)/shard_map/ppermute | solution.py:17
  260.9 37.5 %collective-permute-start.2 = (bf16[320,2560]{1,0:T(8,128)(2,1)}, bf16[320,2560]{1,0:T(8,128)(2,1)}, u32[]{:S(2)}, u32[]{:S(2)}) collective-permute-start(bf16[320,2560]{1,0:T(8,128)(2,1)} %collective-permute-done.1), channel_id=1, source_target_pairs={{0,8},{8,16},{16,24},{24,0},{1,9},{9,17},{17,25},{25,1},{2,10},{10... | collective-permute-start | bytes 4915208 | tf_op jit(solution)/shard_map/ppermute | solution.py:17
  261.5 86.9 %all-gather.8.cloned.1.call-start = ((), (), s32[]{:S(2)}) async-start(), calls=%async_computation.1 | async-start | bytes 2949120 | tf_op jit(solution)/shard_map/all_gather | solution.py:216
  261.8 39.7 %copy-start.3 = (bf16[320,2560]{1,0:T(8,128)(2,1)S(1)}, bf16[320,2560]{1,0:T(8,128)(2,1)}, u32[]{:S(2)}) copy-start(bf16[320,2560]{1,0:T(8,128)(2,1)} %copy-done.2) | copy-start | bytes 4915204
  305.1 4.7 %copy-start.4 = (bf16[2560,2560]{1,0:T(8,128)(2,1)}, bf16[2560,2560]{1,0:T(8,128)(2,1)S(1)}, u32[]{:S(2)}) copy-start(bf16[2560,2560]{1,0:T(8,128)(2,1)S(1)} %constant_dynamic-update-slice_fusion) | copy-start | bytes 39321604
  312.5 145.3 %all-reduce.2.cloned.1.call-start = ((), (), s32[]{:S(2)}) async-start(), calls=%async_computation.3 | async-start | bytes 3276800 | tf_op jit(solution)/shard_map/psum | solution.py:255
  457.7 3.9 copy-start.5
  457.7 3.9 copy-start.6
  457.7 3.9 copy-start.7
Sparse Core Ops, SparseCore 0:
  9.7 36.5 all-gather.9
  47.9 32.8 all-gather.11
  134.2 121.3 reduce-scatter.1
  261.6 32.8 all-gather.13
  312.6 35.7 all-gather.7
  350.7 60.7 all-reduce.1
